TPU v7x, 32 devices: a whole 2x2x4 slice. The times are simulated.
32 devices in a mesh: groups: 2 (over x), pair: 16 (over z, y, core).
Axes of the slice: x: 2, y: 2, z: 4, core: 2. Of those that a mesh axis runs over, the one named last changes fastest.
Arguments:
- t2_amp: float32 [128, 8, 9216], P(('groups', 'pair')), parts along dimension 0, may hold values from -6 to 6
- ladder_ints: bfloat16 [147456, 9216], P(('groups', 'pair')), parts along dimension 0, may hold values from -0.0625 to 0.0625
- fock_vv: float32 [16, 96, 96], P('groups'), parts along dimension 0, may hold values from -0.625 to 0.625
- vir_energy: float32 [16, 96], P('groups'), parts along dimension 0, may hold values from 0.5 to 4
- occ_energy: float32 [300], P('groups'), parts along dimension 0, may hold values from -3 to -0.5
- vir_sizes: int32 [16], P('groups'), parts along dimension 0, may hold values from 48 to 96, as said below
- pair_index: int32 [128, 2], P(('groups', 'pair')), parts along dimension 0, may hold values from 0 to 149, as said below
Outputs:
- increment: float32 [128, 8, 9216], P(('groups', 'pair')), parts along dimension 0
There are 2 independent parts, one for each index of `groups`. A program takes and returns all parts, laid end to end along the dimension named above; each array names one. Nothing has to cross between parts.
Inputs may be any that keep to these rules, and one draw needn't show every extreme that they name: `vir_sizes`: at least one irrep block is full. `pair_index`: each pair has i <= j.
All inputs are finite; a program needn't handle non-finite values.
Results may differ from a plain program's by a relative error of at most 0.0016.
Values may be sent and summed in bfloat16 or wider, within the bound.
No kernel may reach another device: no remote copies, remote signals or barrier semaphores. Data moves between devices by JAX's collectives and lax.ppermute only.
A program may use at most 192 MiB of HBM per device.

v0:
```python
import jax
import jax.numpy as jnp
from jax import lax
from jax.sharding import PartitionSpec as P


def row_product(piece, integrals):
    return lax.dot_general(
        piece, integrals, (((1,), (1,)), ((), ())), preferred_element_type=jnp.float32
    )


def on_device(t2_amp, ladder_ints, fock_vv, vir_energy, occ_energy, vir_sizes, pair_index):
    irreps = vir_energy.shape[0]
    width = vir_energy.shape[1]
    square = width * width
    pair_count = t2_amp.shape[0]
    live = jnp.arange(width, dtype=jnp.int32)[None, :] < vir_sizes[:, None]
    pair_live = (live[:, :, None] & live[:, None, :]).reshape(irreps, square)
    masked = jnp.where(pair_live[None], t2_amp, jnp.zeros_like(t2_amp))
    block = masked[:, 0, :].astype(jnp.bfloat16)
    gathered = lax.all_gather(block, "pair", axis=0, tiled=True)
    ladder = row_product(gathered, ladder_ints)
    ladder = lax.all_to_all(ladder, "pair", split_axis=0, concat_axis=1, tiled=True)
    ladder = ladder.reshape(pair_count, irreps, square)
    amps = masked.reshape(pair_count, irreps, width, width)
    fock = jnp.einsum("phac,hcb->phab", amps, fock_vv, precision=lax.Precision.HIGHEST)
    fock = fock + jnp.einsum("hac,phcb->phab", fock_vv, amps, precision=lax.Precision.HIGHEST)
    fock = fock.reshape(pair_count, irreps, square)
    occupied = occ_energy.shape[0]
    matched = pair_index[:, :, None] == jnp.arange(occupied, dtype=jnp.int32)[None, None, :]
    chosen = jnp.sum(
        jnp.where(matched, occ_energy[None, None, :], jnp.zeros_like(occ_energy)[None, None, :]),
        axis=-1,
    )
    vir_pair = (vir_energy[:, :, None] + vir_energy[:, None, :]).reshape(irreps, square)
    denom = vir_pair[None] - (chosen[:, 0] + chosen[:, 1])[:, None, None]
    total = (ladder + fock) / denom
    return jnp.where(pair_live[None], total, jnp.zeros_like(total))


def solution(mesh):
    in_specs = (
        P(("groups", "pair"), None, None),
        P(("groups", "pair"), None),
        P("groups", None, None),
        P("groups", None),
        P("groups"),
        P("groups"),
        P(("groups", "pair"), None),
    )
    out_specs = P(("groups", "pair"), None, None)
    return jax.shard_map(
        on_device, mesh=mesh, in_specs=in_specs, out_specs=out_specs, check_vma=False
    )
```

profile of v0, /device:TPU:11, one launch (start us, length us, event | category | flops | bytes accessed | tf_op | source)
XLA Modules:
  0.0 133.6 jit_solution(3839741464054956560)
XLA Ops:
  6.5 0.8 iota_compare_fusion.1
  7.3 0.2 broadcast_and_fusion
  7.5 0.3 and.23
  7.8 1.4 %broadcast_select_fusion = f32[4,8,9216]{2,1,0:T(8,128)S(1)} fusion(f32[4,8,9216]{2,1,0:T(8,128)} %param.7, pred[8,9216]{1,0:T(8,128)(4,1)S(1)} %and.23), kind=kLoop, calls=%fused_computation.10 | loop fusion | flops 294912 | bytes 2433024 | tf_op jit(solution)/shard_map/jit(_where)/select_n | solution.py:20
  9.2 0.7 slice.17
  9.9 0.0 all-gather.3.cloned.1.call-update
  10.0 43.4 %all-gather.3.cloned.1.call-done = bf16[64,1,9216]{2,1,0:T(2,128)(2,1)} async-done(((bf16[4,1,9216]{2,1,0:T(2,128)(2,1)}), bf16[64,1,9216]{2,1,0:T(2,128)(2,1)}) %all-gather.3.cloned.1.call-update) | async-done | bytes 1179664 | tf_op jit(solution)/shard_map/all_gather | solution.py:22
  53.4 33.6 %fusion.3 = f32[64,4608]{1,0:T(8,128)S(1)} fusion(bf16[4608,9216]{1,0:T(8,128)(2,1)} %param.8, bf16[64,1,9216]{2,1,0:T(2,128)(2,1)} %all-gather.3.cloned.1.call-done), kind=kOutput, calls=%fused_computation.4 | convolution fusion | flops 5435817984 | bytes 87293952 | tf_op jit(solution)/shard_map/dot_general | solution.py:8
  87.0 1.4 %all_to_all.12 = f32[16,4,4608]{2,1,0:T(4,128)} reshape(f32[64,4608]{1,0:T(8,128)S(1)} %fusion.3) | data formatting | bytes 2359296 | tf_op jit(solution)/shard_map/all_to_all | solution.py:24
  88.3 5.1 %all-to-all-start = ((f32[16,4,4608]{2,1,0:T(4,128)}), f32[16,4,4608]{2,1,0:T(4,128)}, u32[]{:S(2)}, u32[]{:S(2)}) async-start(f32[16,4,4608]{2,1,0:T(4,128)} %all_to_all.12), calls=%async_computation | async-start | bytes 2359296 | tf_op jit(solution)/shard_map/all_to_all | solution.py:24
  93.4 0.6 reshape.93
  94.1 1.5 %fusion.1 = f32[8,4,96,96]{3,2,1,0:T(8,128)S(1)} fusion(f32[4,8,96,96]{3,2,1,0:T(8,128)S(1)} %reshape.93, f32[8,96,96]{2,1,0:T(8,128)S(1)} %copy-done), kind=kOutput, calls=%fused_computation.2 | convolution fusion | flops 339738624 | bytes 2654208 | tf_op jit(solution)/shard_map/phac,hcb->phab/dot_general | solution.py:27
  95.6 1.6 %bitcast_add_fusion = f32[4,8,96,96]{3,2,0,1:T(8,128)S(1)} fusion(f32[8,4,96,96]{3,2,1,0:T(8,128)S(1)} %fusion.1, f32[4,8,96,96]{3,2,1,0:T(8,128)S(1)} %reshape.93, f32[8,96,96]{2,1,0:T(8,128)S(1)} %copy-done), kind=kOutput, calls=%fused_computation | convolution fusion | flops 340033536 | bytes 3833856 | tf_op jit(solution)/shard_map/hac,phcb->phab/dot_general | solution.py:28
  97.2 0.0 copy-start.4
  97.2 0.0 copy-start.5
  97.2 2.2 %reshape.94 = f32[4,8,9216]{2,0,1:T(4,128)} reshape(f32[4,8,96,96]{3,2,0,1:T(8,128)S(1)} %bitcast_add_fusion) | data formatting | bytes 2359296 | tf_op jit(solution)/shard_map/reshape | solution.py:29
  99.4 0.2 broadcast_add_fusion
  99.5 0.2 add.41
  99.8 0.2 select_reduce_fusion
  99.9 21.2 %all-to-all-done = f32[16,4,4608]{2,1,0:T(4,128)} async-done(((f32[16,4,4608]{2,1,0:T(4,128)}), f32[16,4,4608]{2,1,0:T(4,128)}, u32[]{:S(2)}, u32[]{:S(2)}) %all-to-all-start) | async-done | bytes 1179680 | tf_op jit(solution)/shard_map/all_to_all | solution.py:24
  121.1 1.7 %copy.25 = f32[4,16,4608]{2,1,0:T(8,128)S(1)} copy(f32[4,16,4608]{2,0,1:T(4,128)} %bitcast) | data formatting | bytes 2359296 | tf_op jit(solution)/shard_map/all_to_all | solution.py:24
  122.8 0.4 reshape.92
  123.2 0.5 copy-done.2
  123.7 3.1 %fusion.7 = f32[4,8,9216]{2,1,0:T(8,128)} fusion(f32[4,8,9216]{2,1,0:T(8,128)S(1)} %reshape.92, f32[4,8,9216]{2,0,1:T(4,128)} %reshape.94, f32[4]{0:T(128)S(1)} %add_bitcast_fusion, f32[8,9216]{1,0:T(8,128)S(1)} %add.41, pred[8,9216]{1,0:T(8,128)(4,1)S(1)} %copy-done.2), kind=kLoop, calls=%fused_computation.9 | loop fusion | flops 1179648 | bytes 3907600 | tf_op jit(solution)/shard_map/jit(_where)/select_n | solution.py:39
  (11 shorter events, 0.0 us)
Async XLA Ops:
  6.5 87.5 %copy-start = (f32[8,96,96]{2,1,0:T(8,128)S(1)}, f32[8,96,96]{2,1,0:T(8,128)}, u32[]{:S(2)}) copy-start(f32[8,96,96]{2,1,0:T(8,128)} %param.9) | copy-start | bytes 884740
  6.5 46.8 %all-gather.3.cloned.1.call-start = ((), (), s32[]{:S(2)}) async-start(), calls=%async_computation.1 | async-start | bytes 2506752 | tf_op jit(solution)/shard_map/all_gather | solution.py:22
  7.8 1.4 %copy-start.1 = (pred[8,9216]{1,0:T(8,128)(4,1)}, pred[8,9216]{1,0:T(8,128)(4,1)S(1)}, u32[]{:S(2)}) copy-start(pred[8,9216]{1,0:T(8,128)(4,1)S(1)} %and.23) | copy-start | bytes 221188
  88.3 32.8 %all-to-all-start = ((f32[16,4,4608]{2,1,0:T(4,128)}), f32[16,4,4608]{2,1,0:T(4,128)}, u32[]{:S(2)}, u32[]{:S(2)}) async-start(f32[16,4,4608]{2,1,0:T(4,128)} %all_to_all.12), calls=%async_computation | async-start | bytes 2359296 | tf_op jit(solution)/shard_map/all_to_all | solution.py:24
  97.2 2.2 %copy-start.3 = (f32[8,96]{1,0:T(8,128)S(1)}, f32[8,96]{1,0:T(8,128)}, u32[]{:S(2)}) copy-start(f32[8,96]{1,0:T(8,128)} %param.10) | copy-start | bytes 9220
  97.2 2.6 %copy-start.4 = (f32[150]{0:T(256)S(1)}, f32[150]{0:T(256)}, u32[]{:S(2)}) copy-start(f32[150]{0:T(256)} %param.11) | copy-start | bytes 1804
  97.2 2.6 %copy-start.5 = (s32[4,2]{0,1:T(2,128)S(1)}, s32[4,2]{0,1:T(2,128)}, u32[]{:S(2)}) copy-start(s32[4,2]{0,1:T(2,128)} %param.13) | copy-start | bytes 100
  122.8 0.9 copy-start.2
Sparse Core Ops, SparseCore 0:
  10.1 43.2 all-gather.2
where the time goes:
time: 134 us
  waiting for transfers between devices  64.6 us (48%)
  matrix products  36.7 us (27%)
  between operations  13.5 us (10%)
  local copies, waits for them, and re-layouts  7.94 us (6%)
  other arithmetic  5.73 us (4%)
  starting transfers between devices  5.12 us (4%)
    all_gather x1, waiting for transfers between devices, on_device(): gathered = lax.all_gather(block, 'pair', axis=0, tiled=True)  43.4 us
    dot_general x1, matrix products, row_product(): lax.dot_general(piece, integrals, (((1,), (1,)), ((), ())), preferred_ele...  33.6 us
    all_to_all x1, waiting for transfers between devices, on_device(): lax.all_to_all(ladder, 'pair', split_axis=0, concat_axis=1, tiled=True)  21.2 us
    all_to_all x1, starting transfers between devices, on_device(): lax.all_to_all(ladder, 'pair', split_axis=0, concat_axis=1, tiled=True)  5.12 us
    select_n x1, other arithmetic, on_device(): return jnp.where(pair_live[None], total, jnp.zeros_like(total))  3.07 us
    all_to_all x2, local copies, waits for them, and re-layouts, on_device(): lax.all_to_all(ladder, 'pair', split_axis=0, concat_axis=1, tiled=True)  3.01 us
  transfers between devices with their start and end apart: 2, of which 2 were waited for; matrix products, arithmetic and copies ran while one was open for 5% of the time, Pallas kernels for 0%

commit v1 on v0

v1 whole, which is shorter than its diff:
```python
import functools

import jax
import jax.numpy as jnp
from jax import lax
from jax.experimental import pallas as pl
from jax.experimental.pallas import tpu as pltpu
from jax.sharding import PartitionSpec as P

CONTRACT_LAST = (((1,), (1,)), ((), ()))
VMEM_BYTES = 48 * 1024 * 1024


def tile_of(rows, most):
    for size in range(most - most % 128, 0, -128):
        if rows % size == 0:
            return size
    return rows


def pairs_by_core(own_ref, other_ref, amps):
    core = lax.rem(lax.axis_index("pair"), 2)
    count = own_ref.shape[0] * own_ref.shape[1]
    for ref, place in ((own_ref, core), (other_ref, 1 - core)):
        values = ref[...].astype(jnp.float32).reshape(count, ref.shape[2])
        amps[pl.ds(pl.multiple_of(place * count, count), count), :] = values.astype(amps.dtype)


def first_half_kernel(own_ref, other_ref, ints_ref, out_ref, amps):
    @pl.when(pl.program_id(0) == 0)
    def _():
        pairs_by_core(own_ref, other_ref, amps)

    out_ref[...] = lax.dot_general(
        ints_ref[...], amps[...], CONTRACT_LAST, preferred_element_type=jnp.float32
    ).T


def first_half(own, other, ints):
    rows, half = ints.shape[0], own.shape[2]
    pairs = 2 * own.shape[0] * own.shape[1]
    tile = tile_of(rows, 512)
    whole = pl.BlockSpec(own.shape, lambda i: (0, 0, 0))
    return pl.pallas_call(
        first_half_kernel,
        grid=(rows // tile,),
        in_specs=[whole, whole, pl.BlockSpec((tile, half), lambda i: (i, 0))],
        out_specs=pl.BlockSpec((pairs, tile), lambda i: (0, i)),
        out_shape=jax.ShapeDtypeStruct((pairs, rows), jnp.float32),
        scratch_shapes=[pltpu.VMEM((pairs, half), jnp.bfloat16)],
        compiler_params=pltpu.CompilerParams(vmem_limit_bytes=VMEM_BYTES),
        cost_estimate=pl.CostEstimate(
            flops=2 * pairs * rows * half, bytes_accessed=2 * rows * half, transcendentals=0
        ),
        name="first_half",
    )(own, other, ints)


def second_half_kernel(steps_ref, own_ref, other_ref, ints_ref, part_ref, out_ref, amps, slots, total, arrived, *, start):
    depth, tile, width = slots.shape
    tiles = part_ref.shape[1] // tile
    steps = steps_ref[0]
    items = tiles * steps

    def fetch(slot, place, step):
        return pltpu.make_async_copy(
            ints_ref.at[
                pl.ds(pl.multiple_of(start + place * tile, tile), tile),
                pl.ds(pl.multiple_of(amps.shape[1] + step * width, 128), width),
            ],
            slots.at[slot],
            arrived.at[slot],
        )

    def following(place, step):
        wraps = step + 1 == steps
        return jnp.where(wraps, place + 1, place), jnp.where(wraps, 0, step + 1)

    ahead = (jnp.int32(0), jnp.int32(0))
    for slot in range(depth - 1):
        @pl.when(slot < items)
        def _(slot=slot, ahead=ahead):
            fetch(slot, *ahead).start()

        ahead = following(*ahead)
    pairs_by_core(own_ref, other_ref, amps)

    def item(index, state):
        place, step, next_place, next_step = state
        slot = lax.rem(index, depth)
        fetch(slot, place, step).wait()

        @pl.when(index + depth - 1 < items)
        def _():
            fetch(lax.rem(index + depth - 1, depth), next_place, next_step).start()

        columns = pl.ds(pl.multiple_of(step * width, 128), width)
        product = lax.dot_general(
            slots[slot], amps[:, columns], CONTRACT_LAST, preferred_element_type=jnp.float32
        )

        @pl.when(step == 0)
        def _():
            total[...] = product

        @pl.when(step > 0)
        def _():
            total[...] += product

        @pl.when(step == steps - 1)
        def _():
            spot = pl.ds(pl.multiple_of(place * tile, 128), tile)
            ladder = total[...].T + part_ref[:, spot]
            own = out_ref.shape[1]
            chips = out_ref.shape[0] // 2
            for core in range(2):
                for chip in range(chips):
                    first = (core * chips + chip) * own
                    out_ref[2 * chip + core, :, spot] = ladder[first : first + own].astype(out_ref.dtype)

        return (*following(place, step), *following(next_place, next_step))

    lax.fori_loop(0, items, item, (jnp.int32(0), jnp.int32(0), *ahead))


def second_half(own, other, ints, part, live_columns, start, count):
    chips, each, half = own.shape
    pairs = 2 * chips * each
    tile = tile_of(count, 1152)
    stripe = 768
    steps = jnp.maximum((live_columns + stripe - 1) // stripe, 1).reshape(1)
    return pl.pallas_call(
        functools.partial(second_half_kernel, start=start),
        grid_spec=pltpu.PrefetchScalarGridSpec(
            num_scalar_prefetch=1,
            grid=(1,),
            in_specs=[
                pl.BlockSpec(own.shape, lambda i, s: (0, 0, 0)),
                pl.BlockSpec(own.shape, lambda i, s: (0, 0, 0)),
                pl.BlockSpec(memory_space=pl.ANY),
                pl.BlockSpec((pairs, count), lambda i, s: (0, start // count)),
            ],
            out_specs=pl.BlockSpec((2 * chips, each, count), lambda i, s: (0, 0, 0)),
            scratch_shapes=[
                pltpu.VMEM((pairs, half), jnp.bfloat16),
                pltpu.VMEM((4, tile, stripe), jnp.bfloat16),
                pltpu.VMEM((tile, pairs), jnp.float32),
                pltpu.SemaphoreType.DMA((4,)),
            ],
        ),
        out_shape=jax.ShapeDtypeStruct((2 * chips, each, count), jnp.bfloat16),
        compiler_params=pltpu.CompilerParams(vmem_limit_bytes=VMEM_BYTES),
        cost_estimate=pl.CostEstimate(
            flops=2 * pairs * count * half, bytes_accessed=2 * count * half, transcendentals=0
        ),
        name="second_half",
    )(steps, own, other, ints, part)


def on_device(devices, t2_amp, ladder_ints, fock_vv, vir_energy, occ_energy, vir_sizes, pair_index):
    irreps = vir_energy.shape[0]
    width = vir_energy.shape[1]
    square = width * width
    half = square // 2
    pair_count = t2_amp.shape[0]
    rows = ladder_ints.shape[0]
    live = jnp.arange(width, dtype=jnp.int32)[None, :] < vir_sizes[:, None]
    pair_live = (live[:, :, None] & live[:, None, :]).reshape(irreps, square)
    block = jnp.where(pair_live[0][None], t2_amp[:, 0, :], 0.0).astype(jnp.bfloat16)
    same_core = [[2 * chip + core for chip in range(devices // 2)] for core in range(2)]
    other_core = [(device, device ^ 1) for device in range(devices)]

    def gathered(part):
        copies = jnp.broadcast_to(part[None], (devices // 2,) + part.shape)
        own = lax.all_to_all(
            copies, "pair", split_axis=0, concat_axis=0, axis_index_groups=same_core
        )
        return own, lax.ppermute(own, "pair", other_core)

    first = gathered(block[:, :half])
    second = gathered(block[:, half:])
    part = first_half(*first, ladder_ints)
    second_live = (vir_sizes[0] - width // 2) * width
    cuts = 2 if rows % 256 == 0 else 1
    pieces = []
    for piece in range(cuts):
        count = rows // cuts
        sent = second_half(*second, ladder_ints, part, second_live, piece * count, count)
        pieces.append(lax.all_to_all(sent, "pair", split_axis=0, concat_axis=0))
    ladder = jnp.concatenate(pieces, axis=2)
    ladder = jnp.swapaxes(ladder, 0, 1).reshape(pair_count, irreps, square).astype(jnp.float32)

    masked = jnp.where(pair_live[None], t2_amp, jnp.zeros_like(t2_amp))
    amps = masked.reshape(pair_count, irreps, width, width)
    fock = jnp.einsum("phac,hcb->phab", amps, fock_vv, precision=lax.Precision.HIGHEST)
    fock = fock + jnp.einsum("hac,phcb->phab", fock_vv, amps, precision=lax.Precision.HIGHEST)
    fock = fock.reshape(pair_count, irreps, square)
    occupied = occ_energy.shape[0]
    matched = pair_index[:, :, None] == jnp.arange(occupied, dtype=jnp.int32)[None, None, :]
    chosen = jnp.sum(
        jnp.where(matched, occ_energy[None, None, :], jnp.zeros_like(occ_energy)[None, None, :]),
        axis=-1,
    )
    vir_pair = (vir_energy[:, :, None] + vir_energy[:, None, :]).reshape(irreps, square)
    denom = vir_pair[None] - (chosen[:, 0] + chosen[:, 1])[:, None, None]
    total = (ladder + fock) / denom
    return jnp.where(pair_live[None], total, jnp.zeros_like(total))


def solution(mesh):
    in_specs = (
        P(("groups", "pair"), None, None),
        P(("groups", "pair"), None),
        P("groups", None, None),
        P("groups", None),
        P("groups"),
        P("groups"),
        P(("groups", "pair"), None),
    )
    out_specs = P(("groups", "pair"), None, None)
    return jax.shard_map(
        functools.partial(on_device, mesh.shape["pair"]),
        mesh=mesh,
        in_specs=in_specs,
        out_specs=out_specs,
        check_vma=False,
    )
```

time: 134 us -> 110 us (0.82)
  waiting for transfers between devices: 64.6 us -> 12.4 us
  Pallas kernels: 0 us -> 40.6 us
  matrix products: 36.7 us -> 5.77 us
  starting transfers between devices: 5.12 us -> 22.1 us
  between operations: 13.5 us -> 0.26 us
  blocking collectives: 0 us -> 12.8 us
    all_gather x1 -> x0, waiting for transfers between devices: 43.4 us -> none  [on_device(): gathered = lax.all_gather(block, 'pair', axis=0, tiled=True)]
    pallas_call x0 -> x3, Pallas kernels: none -> 40.6 us  [the longest x2 21.4 us: second_half(): pl.pallas_call(functools.partial(second_half_kernel, start=start), grid_s...]
    dot_general x1 -> x0, matrix products: 33.6 us -> none  [row_product(): lax.dot_general(piece, integrals, (((1,), (1,)), ((), ())), preferred_ele...]
    all_to_all x0 -> x1, blocking collectives: none -> 12.8 us  [gathered(): lax.all_to_all(copies, 'pair', split_axis=0, concat_axis=0, axis_index_gr...]
    all_to_all x1 -> x3, starting transfers between devices: 5.12 us -> 16.1 us  [the longest x2 10.4 us: on_device(): pieces.append(lax.all_to_all(sent, 'pair', split_axis=0, concat_axis=0))]
    all_to_all x1 -> x3, waiting for transfers between devices: 21.2 us -> 12.4 us  [the longest x2 8.78 us: on_device(): pieces.append(lax.all_to_all(sent, 'pair', split_axis=0, concat_axis=0))]
    ppermute x0 -> x2, starting transfers between devices: none -> 5.98 us  [gathered(): return (own, lax.ppermute(own, 'pair', other_core))]
    all_to_all x2 -> x0, local copies, waits for them, and re-layouts: 3.01 us -> none  [on_device(): lax.all_to_all(ladder, 'pair', split_axis=0, concat_axis=1, tiled=True)]
  transfers between devices with their start and end apart: 2 -> 5, of which waited for: 2 -> 2; matrix products, arithmetic and copies ran while one was open for 5% -> 12% of each run, Pallas kernels for 0% -> 27%
where the time goes in v1:
time: 110 us; the launch traced here: 109 us
  Pallas kernels  40.6 us (37%)
  starting transfers between devices  22.1 us (20%)
  blocking collectives  12.8 us (12%)
  waiting for transfers between devices  12.4 us (11%)
  local copies, waits for them, and re-layouts  8.83 us (8%)
  other arithmetic  6.02 us (5%)
  matrix products  5.77 us (5%)
    pallas_call x2, Pallas kernels, second_half(): pl.pallas_call(functools.partial(second_half_kernel, start=start), grid_s...  21.4 us
    pallas_call x1, Pallas kernels, first_half(): pl.pallas_call(first_half_kernel, grid=(rows // tile,), in_specs=[whole,...  19.2 us
    all_to_all x1, blocking collectives, gathered(): lax.all_to_all(copies, 'pair', split_axis=0, concat_axis=0, axis_index_gr...  12.8 us
    all_to_all x2, starting transfers between devices, on_device(): pieces.append(lax.all_to_all(sent, 'pair', split_axis=0, concat_axis=0))  10.4 us
    all_to_all x2, waiting for transfers between devices, on_device(): pieces.append(lax.all_to_all(sent, 'pair', split_axis=0, concat_axis=0))  8.78 us
    ppermute x2, starting transfers between devices, gathered(): return (own, lax.ppermute(own, 'pair', other_core))  5.98 us
    all_to_all x1, starting transfers between devices, gathered(): lax.all_to_all(copies, 'pair', split_axis=0, concat_axis=0, axis_index_gr...  5.75 us
    all_to_all x1, waiting for transfers between devices, gathered(): lax.all_to_all(copies, 'pair', split_axis=0, concat_axis=0, axis_index_gr...  3.61 us
  transfers between devices with their start and end apart: 5, of which 2 were waited for; matrix products, arithmetic and copies ran while one was open for 12% of the time, Pallas kernels for 27%

profile of v1, /device:TPU:11, one launch (start us, length us, event | category | flops | bytes accessed | tf_op | source)
XLA Modules:
  0.0 108.8 jit_solution(13623244879793732273)
XLA Ops:
  0.0 0.8 iota_compare_fusion.1
  1.1 1.4 %slice.24 = bf16[4,1,9216]{2,1,0:T(2,128)(2,1)S(1)} slice(f32[4,8,9216]{2,1,0:T(8,128)} %param.7), slice={[0:4], [0:1], [0:9216]} | slice | bytes 147456 | tf_op jit(solution)/shard_map/slice | solution.py:169
  2.6 12.8 %all_to_all.20.own_ref = bf16[8,4,4608]{2,1,0:T(4,128)(2,1)S(1)} all-to-all(bf16[8,4,4608]{2,1,0:T(4,128)(2,1)S(1)} %broadcast_in_dim.68), channel_id=1, replica_groups={{0,2,4,6,8,10,12,14},{1,3,5,7,9,11,13,15},{16,18,20,22,24,26,28,30},{17..., dimensions={0} | all-to-all | bytes 589824 | tf_op jit(solution)/shard_map/all_to_all | solution.py:175
  15.4 0.8 broadcast_in_dim.67
  16.2 5.7 %all-to-all-start = ((bf16[8,4,4608]{2,1,0:T(4,128)(2,1)}), bf16[8,4,4608]{2,1,0:T(4,128)(2,1)S(1)}, u32[]{:S(2)}, u32[]{:S(2)}) async-start(bf16[8,4,4608]{2,1,0:T(4,128)(2,1)} %broadcast_in_dim.67), calls=%async_computation | async-start | bytes 589824 | tf_op jit(solution)/shard_map/all_to_all | solution.py:175
  22.0 0.3 and.28
  22.3 1.9 %collective-permute-start.1 = (bf16[8,4,4608]{2,1,0:T(4,128)(2,1)S(1)}, bf16[8,4,4608]{2,1,0:T(4,128)(2,1)S(1)}, u32[]{:S(2)}, u32[]{:S(2)}) collective-permute-start(bf16[8,4,4608]{2,1,0:T(4,128)(2,1)S(1)} %all_to_all.20.own_ref), channel_id=1, source_target_pairs={{0,1},{1,0},{2,3},{3,2},{4,5},{5,4},{6,7},{7,6},{8,9},{9,8},{10,11... | collective-permute-start | bytes 884744 | tf_op jit(solution)/shard_map/ppermute | solution.py:178
  24.2 3.6 %all-to-all-done.own_ref = bf16[8,4,4608]{2,1,0:T(4,128)(2,1)S(1)} async-done(((bf16[8,4,4608]{2,1,0:T(4,128)(2,1)}), bf16[8,4,4608]{2,1,0:T(4,128)(2,1)S(1)}, u32[]{:S(2)}, u32[]{:S(2)}) %all-to-all-start) | async-done | bytes 294944 | tf_op jit(solution)/shard_map/all_to_all | solution.py:175
  27.8 4.0 %collective-permute-start = (bf16[8,4,4608]{2,1,0:T(4,128)(2,1)S(1)}, bf16[8,4,4608]{2,1,0:T(4,128)(2,1)S(1)}, u32[]{:S(2)}, u32[]{:S(2)}) collective-permute-start(bf16[8,4,4608]{2,1,0:T(4,128)(2,1)S(1)} %all-to-all-done.own_ref), channel_id=1, source_target_pairs={{0,1},{1,0},{2,3},{3,2},{4,5},{5,4},{6,7},{7,6},{8,9},{9,8},{10,11... | collective-permute-start | bytes 884744 | tf_op jit(solution)/shard_map/ppermute | solution.py:178
  31.9 1.4 %broadcast_select_fusion = f32[4,8,9216]{2,1,0:T(8,128)S(1)} fusion(f32[4,8,9216]{2,1,0:T(8,128)} %param.7, pred[8,9216]{1,0:T(8,128)(4,1)S(1)} %and.28), kind=kLoop, calls=%fused_computation.8 | loop fusion | flops 294912 | bytes 2433024 | tf_op jit(solution)/shard_map/jit(_where)/select_n | solution.py:193
  33.3 1.8 %reshape.108 = f32[4,8,96,96]{3,2,1,0:T(8,128)} reshape(f32[4,8,9216]{2,1,0:T(8,128)S(1)} %broadcast_select_fusion) | data formatting | bytes 2359296 | tf_op jit(solution)/shard_map/reshape | solution.py:194
  35.1 19.2 %first_half.1.part_ref = f32[64,4608]{1,0:T(8,128)S(1)} custom-call(bf16[8,4,4608]{2,1,0:T(4,128)(2,1)S(1)} %all_to_all.20.own_ref, bf16[8,4,4608]{2,1,0:T(4,128)(2,1)S(1)} %collective-permute-done.1.other_ref, bf16[4608,9216]{1,0:T(8,128)(2,1)} %ints_ref.5), custom_call_target="tpu_custom_call" | custom-call | flops 2717908992 | bytes 42467328 | tf_op jit(solution)/shard_map/first_half/pallas_call | solution.py:44
  54.3 10.7 %second_half.2 = bf16[16,4,2304]{2,1,0:T(4,128)(2,1)} custom-call(s32[1]{0:T(128)} %bitcast.2.steps_ref, bf16[8,4,4608]{2,1,0:T(4,128)(2,1)S(1)} %all-to-all-done.own_ref, bf16[8,4,4608]{2,1,0:T(4,128)(2,1)S(1)} %collective-permute-done.other_ref, bf16[4608,9216]{1,0:T(8,128)(2,1)} %ints_ref.5, f32[64,4608]{1,0:T(8,128)S(1)} %first_half.1.part_ref), custom_call_target="tpu_custom_call" | custom-call | flops 1358954496 | bytes 21233664 | tf_op jit(solution)/shard_map/second_half/pallas_call | solution.py:132
  65.0 4.3 %all-to-all-start.2 = ((bf16[16,4,2304]{2,1,0:T(4,128)(2,1)}), bf16[16,4,2304]{2,1,0:T(4,128)(2,1)S(1)}, u32[]{:S(2)}, u32[]{:S(2)}) async-start(bf16[16,4,2304]{2,1,0:T(4,128)(2,1)} %second_half.2), calls=%async_computation.2 | async-start | bytes 589824 | tf_op jit(solution)/shard_map/all_to_all | solution.py:189
  69.4 3.0 %fusion.1 = f32[8,4,96,96]{3,2,1,0:T(8,128)S(1)} fusion(f32[4,8,96,96]{3,2,1,0:T(8,128)} %reshape.108, f32[8,96,96]{2,1,0:T(8,128)S(1)} %copy-done), kind=kOutput, calls=%fused_computation.2 | convolution fusion | flops 339738624 | bytes 2654208 | tf_op jit(solution)/shard_map/phac,hcb->phab/dot_general | solution.py:195
  72.4 2.7 %bitcast_add_fusion = f32[4,8,96,96]{3,2,0,1:T(8,128)} fusion(f32[8,4,96,96]{3,2,1,0:T(8,128)S(1)} %fusion.1, f32[4,8,96,96]{3,2,1,0:T(8,128)S(1)} %copy-done.1, f32[8,96,96]{2,1,0:T(8,128)S(1)} %copy-done), kind=kOutput, calls=%fused_computation | convolution fusion | flops 340033536 | bytes 3833856 | tf_op jit(solution)/shard_map/hac,phcb->phab/dot_general | solution.py:196
  75.2 3.4 %reshape.109 = f32[4,8,9216]{2,0,1:T(4,128)} reshape(f32[4,8,96,96]{3,2,0,1:T(8,128)} %bitcast_add_fusion) | data formatting | bytes 2359296 | tf_op jit(solution)/shard_map/reshape | solution.py:197
  78.5 10.7 %second_half.3 = bf16[16,4,2304]{2,1,0:T(4,128)(2,1)} custom-call(s32[1]{0:T(128)} %bitcast.2.steps_ref, bf16[8,4,4608]{2,1,0:T(4,128)(2,1)S(1)} %all-to-all-done.own_ref, bf16[8,4,4608]{2,1,0:T(4,128)(2,1)S(1)} %collective-permute-done.other_ref, bf16[4608,9216]{1,0:T(8,128)(2,1)} %ints_ref.5, f32[64,4608]{1,0:T(8,128)S(1)} %first_half.1.part_ref), custom_call_target="tpu_custom_call" | custom-call | flops 1358954496 | bytes 21233664 | tf_op jit(solution)/shard_map/second_half/pallas_call | solution.py:132
  89.3 6.0 %all-to-all-start.3 = ((bf16[16,4,2304]{2,1,0:T(4,128)(2,1)}), bf16[16,4,2304]{2,1,0:T(4,128)(2,1)S(1)}, u32[]{:S(2)}, u32[]{:S(2)}) async-start(bf16[16,4,2304]{2,1,0:T(4,128)(2,1)} %second_half.3), calls=%async_computation.3 | async-start | bytes 589824 | tf_op jit(solution)/shard_map/all_to_all | solution.py:189
  95.9 8.8 %all-to-all-done.3 = bf16[16,4,2304]{2,1,0:T(4,128)(2,1)S(1)} async-done(((bf16[16,4,2304]{2,1,0:T(4,128)(2,1)}), bf16[16,4,2304]{2,1,0:T(4,128)(2,1)S(1)}, u32[]{:S(2)}, u32[]{:S(2)}) %all-to-all-start.3) | async-done | bytes 294944 | tf_op jit(solution)/shard_map/all_to_all | solution.py:189
  104.7 0.3 convert_bitcast_fusion
  104.9 0.4 copy.19
  105.3 0.4 reshape.114
  105.7 3.1 %fusion.4 = f32[4,8,9216]{2,1,0:T(8,128)} fusion(f32[4,8,9216]{2,1,0:T(8,128)S(1)} %reshape.114, f32[4,8,9216]{2,0,1:T(4,128)} %reshape.109, f32[4]{0:T(128)S(1)} %add_bitcast_fusion, f32[8,9216]{1,0:T(8,128)S(1)} %add.50, pred[8,9216]{1,0:T(8,128)(4,1)S(1)} %and.28), kind=kLoop, calls=%fused_computation.6 | loop fusion | flops 1179648 | bytes 3907600 | tf_op jit(solution)/shard_map/jit(_where)/select_n | solution.py:207
  (25 shorter events, 1.0 us)
Async XLA Ops:
  0.0 69.4 %copy-start = (f32[8,96,96]{2,1,0:T(8,128)S(1)}, f32[8,96,96]{2,1,0:T(8,128)}, u32[]{:S(2)}) copy-start(f32[8,96,96]{2,1,0:T(8,128)} %param.9) | copy-start | bytes 884740
  16.2 11.6 %all-to-all-start = ((bf16[8,4,4608]{2,1,0:T(4,128)(2,1)}), bf16[8,4,4608]{2,1,0:T(4,128)(2,1)S(1)}, u32[]{:S(2)}, u32[]{:S(2)}) async-start(bf16[8,4,4608]{2,1,0:T(4,128)(2,1)} %broadcast_in_dim.67), calls=%async_computation | async-start | bytes 589824 | tf_op jit(solution)/shard_map/all_to_all | solution.py:175
  22.3 11.0 %copy-start.5 = (s32[8]{0:T(128)S(1)}, s32[8]{0:T(128)}, u32[]{:S(2)}) copy-start(s32[8]{0:T(128)} %param.12) | copy-start | bytes 100
  22.3 12.8 %collective-permute-start.1 = (bf16[8,4,4608]{2,1,0:T(4,128)(2,1)S(1)}, bf16[8,4,4608]{2,1,0:T(4,128)(2,1)S(1)}, u32[]{:S(2)}, u32[]{:S(2)}) collective-permute-start(bf16[8,4,4608]{2,1,0:T(4,128)(2,1)S(1)} %all_to_all.20.own_ref), channel_id=1, source_target_pairs={{0,1},{1,0},{2,3},{3,2},{4,5},{5,4},{6,7},{7,6},{8,9},{9,8},{10,11... | collective-permute-start | bytes 884744 | tf_op jit(solution)/shard_map/ppermute | solution.py:178
  27.8 26.4 %collective-permute-start = (bf16[8,4,4608]{2,1,0:T(4,128)(2,1)S(1)}, bf16[8,4,4608]{2,1,0:T(4,128)(2,1)S(1)}, u32[]{:S(2)}, u32[]{:S(2)}) collective-permute-start(bf16[8,4,4608]{2,1,0:T(4,128)(2,1)S(1)} %all-to-all-done.own_ref), channel_id=1, source_target_pairs={{0,1},{1,0},{2,3},{3,2},{4,5},{5,4},{6,7},{7,6},{8,9},{9,8},{10,11... | collective-permute-start | bytes 884744 | tf_op jit(solution)/shard_map/ppermute | solution.py:178
  65.0 24.3 %all-to-all-start.2 = ((bf16[16,4,2304]{2,1,0:T(4,128)(2,1)}), bf16[16,4,2304]{2,1,0:T(4,128)(2,1)S(1)}, u32[]{:S(2)}, u32[]{:S(2)}) async-start(bf16[16,4,2304]{2,1,0:T(4,128)(2,1)} %second_half.2), calls=%async_computation.2 | async-start | bytes 589824 | tf_op jit(solution)/shard_map/all_to_all | solution.py:189
  69.4 3.1 %copy-start.1 = (f32[4,8,96,96]{3,2,1,0:T(8,128)S(1)}, f32[4,8,96,96]{3,2,1,0:T(8,128)}, u32[]{:S(2)}) copy-start(f32[4,8,96,96]{3,2,1,0:T(8,128)} %reshape.108) | copy-start | bytes 3538948
  78.5 16.8 %copy-start.2 = (f32[8,96]{1,0:T(8,128)S(1)}, f32[8,96]{1,0:T(8,128)}, u32[]{:S(2)}) copy-start(f32[8,96]{1,0:T(8,128)} %param.10) | copy-start | bytes 9220
  89.3 6.5 %copy-start.3 = (f32[150]{0:T(256)S(1)}, f32[150]{0:T(256)}, u32[]{:S(2)}) copy-start(f32[150]{0:T(256)} %param.11) | copy-start | bytes 1804
  89.3 6.4 %copy-start.4 = (s32[4,2]{0,1:T(2,128)S(1)}, s32[4,2]{0,1:T(2,128)}, u32[]{:S(2)}) copy-start(s32[4,2]{0,1:T(2,128)} %param.13) | copy-start | bytes 100
  89.3 15.4 %all-to-all-start.3 = ((bf16[16,4,2304]{2,1,0:T(4,128)(2,1)}), bf16[16,4,2304]{2,1,0:T(4,128)(2,1)S(1)}, u32[]{:S(2)}, u32[]{:S(2)}) async-start(bf16[16,4,2304]{2,1,0:T(4,128)(2,1)} %second_half.3), calls=%async_computation.3 | async-start | bytes 589824 | tf_op jit(solution)/shard_map/all_to_all | solution.py:189

commit v2 on v1

v2 whole, which is shorter than its diff:
```python
import functools

import jax
import jax.numpy as jnp
from jax import lax
from jax.experimental import pallas as pl
from jax.experimental.pallas import tpu as pltpu
from jax.sharding import PartitionSpec as P

CONTRACT_LAST = (((1,), (1,)), ((), ()))
VMEM_BYTES = 48 * 1024 * 1024


def tile_of(rows, most):
    for size in range(most - most % 128, 0, -128):
        if rows % size == 0:
            return size
    return rows


def pairs_by_core(own_ref, other_ref, amps):
    core = lax.rem(lax.axis_index("pair"), 2)
    count = own_ref.shape[0] * own_ref.shape[1]
    for ref, place in ((own_ref, core), (other_ref, 1 - core)):
        values = ref[...].astype(jnp.float32).reshape(count, ref.shape[2])
        amps[pl.ds(pl.multiple_of(place * count, count), count), :] = values.astype(amps.dtype)


def ladder_kernel(steps_ref, own_ref, other_ref, ints_ref, out_ref, amps, slots, total, arrived):
    depth, tile, width = slots.shape
    tiles = out_ref.shape[2] // tile
    steps = steps_ref[0]
    items = tiles * steps

    def fetch(slot, place, step):
        return pltpu.make_async_copy(
            ints_ref.at[
                pl.ds(pl.multiple_of(place * tile, tile), tile),
                pl.ds(pl.multiple_of(step * width, 128), width),
            ],
            slots.at[slot],
            arrived.at[slot],
        )

    def following(place, step):
        wraps = step + 1 == steps
        return jnp.where(wraps, place + 1, place), jnp.where(wraps, 0, step + 1)

    ahead = (jnp.int32(0), jnp.int32(0))
    for slot in range(depth - 1):
        @pl.when(slot < items)
        def _(slot=slot, ahead=ahead):
            fetch(slot, *ahead).start()

        ahead = following(*ahead)
    pairs_by_core(own_ref, other_ref, amps)

    def item(index, state):
        place, step, next_place, next_step = state
        slot = lax.rem(index, depth)
        fetch(slot, place, step).wait()

        @pl.when(index + depth - 1 < items)
        def _():
            fetch(lax.rem(index + depth - 1, depth), next_place, next_step).start()

        columns = pl.ds(pl.multiple_of(step * width, 128), width)
        product = lax.dot_general(
            slots[slot], amps[:, columns], CONTRACT_LAST, preferred_element_type=jnp.float32
        )

        @pl.when(step == 0)
        def _():
            total[...] = product

        @pl.when(step > 0)
        def _():
            total[...] += product

        @pl.when(step == steps - 1)
        def _():
            spot = pl.ds(pl.multiple_of(place * tile, 128), tile)
            ladder = total[...].T
            own = out_ref.shape[1]
            chips = out_ref.shape[0] // 2
            for core in range(2):
                for chip in range(chips):
                    first = (core * chips + chip) * own
                    out_ref[2 * chip + core, :, spot] = ladder[first : first + own].astype(out_ref.dtype)

        return (*following(place, step), *following(next_place, next_step))

    lax.fori_loop(0, items, item, (jnp.int32(0), jnp.int32(0), *ahead))


def ladder_rows(own, other, ints, live_columns):
    chips, each, columns = own.shape
    rows = ints.shape[0]
    pairs = 2 * chips * each
    tile = tile_of(rows, 1152)
    stripe = 768
    steps = jnp.maximum((live_columns + stripe - 1) // stripe, 1).reshape(1)
    return pl.pallas_call(
        ladder_kernel,
        grid_spec=pltpu.PrefetchScalarGridSpec(
            num_scalar_prefetch=1,
            grid=(1,),
            in_specs=[
                pl.BlockSpec(own.shape, lambda i, s: (0, 0, 0)),
                pl.BlockSpec(own.shape, lambda i, s: (0, 0, 0)),
                pl.BlockSpec(memory_space=pl.ANY),
            ],
            out_specs=pl.BlockSpec((2 * chips, each, rows), lambda i, s: (0, 0, 0)),
            scratch_shapes=[
                pltpu.VMEM((pairs, columns), jnp.bfloat16),
                pltpu.VMEM((4, tile, stripe), jnp.bfloat16),
                pltpu.VMEM((tile, pairs), jnp.float32),
                pltpu.SemaphoreType.DMA((4,)),
            ],
        ),
        out_shape=jax.ShapeDtypeStruct((2 * chips, each, rows), jnp.bfloat16),
        compiler_params=pltpu.CompilerParams(vmem_limit_bytes=VMEM_BYTES),
        cost_estimate=pl.CostEstimate(
            flops=2 * pairs * rows * columns, bytes_accessed=2 * rows * columns, transcendentals=0
        ),
        name="ladder_rows",
    )(steps, own, other, ints)


def on_device(devices, t2_amp, ladder_ints, fock_vv, vir_energy, occ_energy, vir_sizes, pair_index):
    irreps = vir_energy.shape[0]
    width = vir_energy.shape[1]
    square = width * width
    pair_count = t2_amp.shape[0]
    live = jnp.arange(width, dtype=jnp.int32)[None, :] < vir_sizes[:, None]
    pair_live = (live[:, :, None] & live[:, None, :]).reshape(irreps, square)
    block = jnp.where(pair_live[0][None], t2_amp[:, 0, :], 0.0).astype(jnp.bfloat16)
    same_core = [[2 * chip + core for chip in range(devices // 2)] for core in range(2)]
    other_core = [(device, device ^ 1) for device in range(devices)]

    copies = jnp.broadcast_to(block[None], (devices // 2,) + block.shape)
    own = lax.all_to_all(
        copies, "pair", split_axis=0, concat_axis=0, axis_index_groups=same_core
    )
    masked = jnp.where(pair_live[None], t2_amp, jnp.zeros_like(t2_amp))
    amps = masked.reshape(pair_count, irreps, width, width)
    fock = jnp.einsum("phac,hcb->phab", amps, fock_vv, precision=lax.Precision.HIGHEST)
    own, amps, fock = lax.optimization_barrier((own, amps, fock))
    other = lax.ppermute(own, "pair", other_core)
    sent = ladder_rows(own, other, ladder_ints, vir_sizes[0] * width)
    sent, amps, fock = lax.optimization_barrier((sent, amps, fock))
    ladder = lax.all_to_all(sent, "pair", split_axis=0, concat_axis=0)
    ladder = jnp.swapaxes(ladder, 0, 1).reshape(pair_count, irreps, square).astype(jnp.float32)
    fock = fock + jnp.einsum("hac,phcb->phab", fock_vv, amps, precision=lax.Precision.HIGHEST)
    fock = fock.reshape(pair_count, irreps, square)
    occupied = occ_energy.shape[0]
    matched = pair_index[:, :, None] == jnp.arange(occupied, dtype=jnp.int32)[None, None, :]
    chosen = jnp.sum(
        jnp.where(matched, occ_energy[None, None, :], jnp.zeros_like(occ_energy)[None, None, :]),
        axis=-1,
    )
    vir_pair = (vir_energy[:, :, None] + vir_energy[:, None, :]).reshape(irreps, square)
    denom = vir_pair[None] - (chosen[:, 0] + chosen[:, 1])[:, None, None]
    total = (ladder + fock) / denom
    return jnp.where(pair_live[None], total, jnp.zeros_like(total))


def solution(mesh):
    in_specs = (
        P(("groups", "pair"), None, None),
        P(("groups", "pair"), None),
        P("groups", None, None),
        P("groups", None),
        P("groups"),
        P("groups"),
        P(("groups", "pair"), None),
    )
    out_specs = P(("groups", "pair"), None, None)
    return jax.shard_map(
        functools.partial(on_device, mesh.shape["pair"]),
        mesh=mesh,
        in_specs=in_specs,
        out_specs=out_specs,
        check_vma=False,
    )
```

time: 110 us -> 87.9 us (0.80)
  the two profiles are of different devices: /device:TPU:11 before, /device:TPU:0 now
where the time goes in v2:
time: 87.9 us; the launch traced here: 87.4 us
  Pallas kernels  35.3 us (40%)
  waiting for transfers between devices  22.9 us (26%)
  starting transfers between devices  11.2 us (13%)
  local copies, waits for them, and re-layouts  7.79 us (9%)
  other arithmetic  5.79 us (7%)
  matrix products  4.17 us (5%)
    pallas_call x1, Pallas kernels, ladder_rows(): pl.pallas_call(ladder_kernel, grid_spec=pltpu.PrefetchScalarGridSpec(num_...  35.3 us
    all_to_all x1, waiting for transfers between devices, on_device(): ladder = lax.all_to_all(sent, 'pair', split_axis=0, concat_axis=0)  11 us
    all_to_all x1, waiting for transfers between devices, on_device(): lax.all_to_all(copies, 'pair', split_axis=0, concat_axis=0, axis_index_gr...  9.92 us
    all_to_all x1, starting transfers between devices, on_device(): lax.all_to_all(copies, 'pair', split_axis=0, concat_axis=0, axis_index_gr...  7.28 us
    all_to_all x1, starting transfers between devices, on_device(): ladder = lax.all_to_all(sent, 'pair', split_axis=0, concat_axis=0)  3.89 us
    select_n x1, other arithmetic, on_device(): return jnp.where(pair_live[None], total, jnp.zeros_like(total))  3.07 us
    dot_general x1, matrix products, on_device(): jnp.einsum('phac,hcb->phab', amps, fock_vv, precision=lax.Precision.HIGHEST)  2.65 us
    reshape x1, local copies, waits for them, and re-layouts, on_device(): fock = fock.reshape(pair_count, irreps, square)  2.16 us
  transfers between devices with their start and end apart: 3, of which 3 were waited for; matrix products, arithmetic and copies ran while one was open for 12% of the time, Pallas kernels for 0%

profile of v2, /device:TPU:0, one launch (start us, length us, event | category | flops | bytes accessed | tf_op | source)
XLA Modules:
  0.0 87.4 jit_solution(14337228512174168315)
XLA Ops:
  0.0 0.8 iota_compare_fusion.1
  0.8 0.2 broadcast_and_fusion
  1.0 0.1 broadcast_in_dim.58
  1.1 1.4 %slice.18 = bf16[4,1,9216]{2,1,0:T(2,128)(2,1)S(1)} slice(f32[4,8,9216]{2,1,0:T(8,128)} %param.7), slice={[0:4], [0:1], [0:9216]} | slice | bytes 147456 | tf_op jit(solution)/shard_map/slice | solution.py:137
  2.5 1.0 %broadcast_in_dim.61 = bf16[8,4,9216]{2,1,0:T(4,128)(2,1)} broadcast(bf16[4,9216]{1,0:T(4,128)(2,1)S(1)} %fusion.11), dimensions={1,2} | broadcast | bytes 663552 | tf_op jit(solution)/shard_map/broadcast_in_dim | solution.py:141
  3.5 7.3 %all-to-all-start = ((bf16[8,4,9216]{2,1,0:T(4,128)(2,1)}), bf16[8,4,9216]{2,1,0:T(4,128)(2,1)S(1)}, u32[]{:S(2)}, u32[]{:S(2)}) async-start(bf16[8,4,9216]{2,1,0:T(4,128)(2,1)} %broadcast_in_dim.61), calls=%async_computation | async-start | bytes 1179648 | tf_op jit(solution)/shard_map/all_to_all | solution.py:142
  10.8 0.3 and.27
  11.1 1.1 %broadcast_select_fusion = f32[4,8,9216]{2,1,0:T(8,128)} fusion(f32[4,8,9216]{2,1,0:T(8,128)S(1)} %copy-done.2, pred[8,9216]{1,0:T(8,128)(4,1)S(1)} %and.27), kind=kLoop, calls=%fused_computation.10 | loop fusion | flops 294912 | bytes 2433024 | tf_op jit(solution)/shard_map/jit(_where)/select_n | solution.py:145
  12.2 1.9 %reshape.130 = f32[4,8,96,96]{3,2,1,0:T(8,128)S(1)} reshape(f32[4,8,9216]{2,1,0:T(8,128)} %broadcast_select_fusion) | data formatting | bytes 2359296 | tf_op jit(solution)/shard_map/reshape | solution.py:146
  14.1 2.6 %fusion.4 = f32[4,8,96,96]{3,2,0,1:T(8,128)} fusion(f32[4,8,96,96]{3,2,1,0:T(8,128)S(1)} %reshape.130, f32[8,96,96]{2,1,0:T(8,128)S(1)} %copy-done), kind=kOutput, calls=%fused_computation.5 | convolution fusion | flops 339738624 | bytes 2654208 | tf_op jit(solution)/shard_map/phac,hcb->phab/dot_general | solution.py:147
  16.8 9.9 %all-to-all-done.own_ref = bf16[8,4,9216]{2,1,0:T(4,128)(2,1)S(1)} async-done(((bf16[8,4,9216]{2,1,0:T(4,128)(2,1)}), bf16[8,4,9216]{2,1,0:T(4,128)(2,1)S(1)}, u32[]{:S(2)}, u32[]{:S(2)}) %all-to-all-start) | async-done | bytes 589856 | tf_op jit(solution)/shard_map/all_to_all | solution.py:142
  26.7 1.9 %collective-permute-done.other_ref = bf16[8,4,9216]{2,1,0:T(4,128)(2,1)S(1)} collective-permute-done((bf16[8,4,9216]{2,1,0:T(4,128)(2,1)S(1)}, bf16[8,4,9216]{2,1,0:T(4,128)(2,1)S(1)}, u32[]{:S(2)}, u32[]{:S(2)}) %collective-permute-start) | collective-permute-done | bytes 589856 | tf_op jit(solution)/shard_map/ppermute | solution.py:149
  28.7 35.3 %ladder_rows.1 = bf16[16,4,4608]{2,1,0:T(4,128)(2,1)} custom-call(s32[1]{0:T(128)} %bitcast.2.steps_ref, bf16[8,4,9216]{2,1,0:T(4,128)(2,1)S(1)} %all-to-all-done.own_ref, bf16[8,4,9216]{2,1,0:T(4,128)(2,1)S(1)} %collective-permute-done.other_ref, bf16[4608,9216]{1,0:T(8,128)(2,1)} %ints_ref.1), custom_call_target="tpu_custom_call" | custom-call | flops 5435817984 | bytes 84934656 | tf_op jit(solution)/shard_map/ladder_rows/pallas_call | solution.py:103
  64.1 3.9 %all-to-all-start.1 = ((bf16[16,4,4608]{2,1,0:T(4,128)(2,1)}), bf16[16,4,4608]{2,1,0:T(4,128)(2,1)S(1)}, u32[]{:S(2)}, u32[]{:S(2)}) async-start(bf16[16,4,4608]{2,1,0:T(4,128)(2,1)} %ladder_rows.1), calls=%async_computation.1 | async-start | bytes 1179648 | tf_op jit(solution)/shard_map/all_to_all | solution.py:152
  68.0 0.2 broadcast_add_fusion
  68.1 0.2 add.47
  68.4 0.2 select_reduce_fusion
  68.5 1.5 %fusion = f32[8,4,96,96]{2,3,1,0:T(8,128)S(1)} fusion(f32[4,8,96,96]{3,2,1,0:T(8,128)S(1)} %reshape.130, f32[8,96,96]{2,1,0:T(8,128)S(1)} %copy-done), kind=kOutput, calls=%fused_computation.1 | convolution fusion | flops 339738624 | bytes 2654208 | tf_op jit(solution)/shard_map/hac,phcb->phab/dot_general | solution.py:154
  70.1 0.2 bitcast_add_fusion
  70.3 2.2 %reshape.131 = f32[4,8,9216]{2,0,1:T(4,128)} reshape(f32[4,8,96,96]{3,2,0,1:T(8,128)S(1)} %bitcast_add_fusion) | data formatting | bytes 2359296 | tf_op jit(solution)/shard_map/reshape | solution.py:155
  72.5 11.0 %all-to-all-done.1 = bf16[16,4,4608]{2,1,0:T(4,128)(2,1)S(1)} async-done(((bf16[16,4,4608]{2,1,0:T(4,128)(2,1)}), bf16[16,4,4608]{2,1,0:T(4,128)(2,1)S(1)}, u32[]{:S(2)}, u32[]{:S(2)}) %all-to-all-start.1) | async-done | bytes 589856 | tf_op jit(solution)/shard_map/all_to_all | solution.py:152
  83.6 0.4 copy.20
  84.0 0.4 reshape.133
  84.4 3.1 %fusion.8 = f32[4,8,9216]{2,1,0:T(8,128)} fusion(f32[4,8,9216]{2,1,0:T(8,128)S(1)} %reshape.133, f32[4,8,9216]{2,0,1:T(4,128)} %reshape.131, f32[4]{0:T(128)S(1)} %add_bitcast_fusion, f32[8,9216]{1,0:T(8,128)S(1)} %add.47, pred[8,9216]{1,0:T(8,128)(4,1)S(1)} %and.27), kind=kLoop, calls=%fused_computation.8 | loop fusion | flops 1179648 | bytes 3907600 | tf_op jit(solution)/shard_map/jit(_where)/select_n | solution.py:165
  (19 shorter events, 0.2 us)
Async XLA Ops:
  0.0 14.1 %copy-start = (f32[8,96,96]{2,1,0:T(8,128)S(1)}, f32[8,96,96]{2,1,0:T(8,128)}, u32[]{:S(2)}) copy-start(f32[8,96,96]{2,1,0:T(8,128)} %param.9) | copy-start | bytes 884740
  2.4 8.6 %copy-start.2 = (f32[4,8,9216]{2,1,0:T(8,128)S(1)}, f32[4,8,9216]{2,1,0:T(8,128)}, u32[]{:S(2)}) copy-start(f32[4,8,9216]{2,1,0:T(8,128)} %param.7) | copy-start | bytes 3538948
  3.5 23.2 %all-to-all-start = ((bf16[8,4,9216]{2,1,0:T(4,128)(2,1)}), bf16[8,4,9216]{2,1,0:T(4,128)(2,1)S(1)}, u32[]{:S(2)}, u32[]{:S(2)}) async-start(bf16[8,4,9216]{2,1,0:T(4,128)(2,1)} %broadcast_in_dim.61), calls=%async_computation | async-start | bytes 1179648 | tf_op jit(solution)/shard_map/all_to_all | solution.py:142
  14.1 12.6 %copy-start.6 = (s32[8]{0:T(128)S(1)}, s32[8]{0:T(128)}, u32[]{:S(2)}) copy-start(s32[8]{0:T(128)} %param.12) | copy-start | bytes 100
  26.7 2.0 %collective-permute-start = (bf16[8,4,9216]{2,1,0:T(4,128)(2,1)S(1)}, bf16[8,4,9216]{2,1,0:T(4,128)(2,1)S(1)}, u32[]{:S(2)}, u32[]{:S(2)}) collective-permute-start(bf16[8,4,9216]{2,1,0:T(4,128)(2,1)S(1)} %all-to-all-done.own_ref), channel_id=1, source_target_pairs={{0,1},{1,0},{2,3},{3,2},{4,5},{5,4},{6,7},{7,6},{8,9},{9,8},{10,11... | collective-permute-start | bytes 1769480 | tf_op jit(solution)/shard_map/ppermute | solution.py:149
  64.0 3.9 %copy-start.3 = (f32[8,96]{1,0:T(8,128)S(1)}, f32[8,96]{1,0:T(8,128)}, u32[]{:S(2)}) copy-start(f32[8,96]{1,0:T(8,128)} %param.10) | copy-start | bytes 9220
  64.0 4.3 %copy-start.4 = (f32[150]{0:T(256)S(1)}, f32[150]{0:T(256)}, u32[]{:S(2)}) copy-start(f32[150]{0:T(256)} %param.11) | copy-start | bytes 1804
  64.0 4.3 %copy-start.5 = (s32[4,2]{0,1:T(2,128)S(1)}, s32[4,2]{0,1:T(2,128)}, u32[]{:S(2)}) copy-start(s32[4,2]{0,1:T(2,128)} %param.13) | copy-start | bytes 100
  64.1 19.4 %all-to-all-start.1 = ((bf16[16,4,4608]{2,1,0:T(4,128)(2,1)}), bf16[16,4,4608]{2,1,0:T(4,128)(2,1)S(1)}, u32[]{:S(2)}, u32[]{:S(2)}) async-start(bf16[16,4,4608]{2,1,0:T(4,128)(2,1)} %ladder_rows.1), calls=%async_computation.1 | async-start | bytes 1179648 | tf_op jit(solution)/shard_map/all_to_all | solution.py:152
  68.5 1.5 %copy-start.1 = (f32[4,8,96,96]{3,2,0,1:T(8,128)S(1)}, f32[4,8,96,96]{3,2,0,1:T(8,128)}, u32[]{:S(2)}) copy-start(f32[4,8,96,96]{3,2,0,1:T(8,128)} %fusion.4) | copy-start | bytes 3538948
